TPU v7x, 256 devices: a whole 4x4x8 slice. The times are simulated.
256 devices in a mesh: row: 32 (over z, x), col: 8 (over y, core).
Axes of the slice: x: 4, y: 4, z: 8, core: 2. Of those that a mesh axis runs over, the one named last changes fastest.
Arguments:
- gate_pre: bfloat16 [4096, 16384], P('col', 'row'), may hold values from -6 to 6
- up_pre: bfloat16 [4096, 16384], P('col', 'row'), may hold values from -6 to 6
- weight: bfloat16 [16384, 8192], P('row', 'col'), may hold values from -0.0625 to 0.0625
- block_mask: int32 [128, 64], P('row', 'col'), may hold values from 0 to 1, as said below
- grad_out: bfloat16 [4096, 8192], P('row', 'col'), may hold values from -6 to 6
Outputs:
- output: bfloat16 [4096, 8192], P('row', 'col')
- grad_gate: bfloat16 [4096, 16384], P('col', 'row')
- grad_up: bfloat16 [4096, 16384], P('col', 'row')
- grad_weight: bfloat16 [16384, 8192], P('row', 'col')
Inputs may be any that keep to these rules, and one draw needn't show every extreme that they name: `block_mask`: exactly half of the blocks are kept; block rows 2m and 2m + 1 together keep 64 blocks, each of them between 8 and 56 blocks.
All inputs are finite; a program needn't handle non-finite values.
Results may differ from a plain program's by a relative error of at most 0.02.
Values may be sent and summed in bfloat16 or wider, within the bound.
A program may use at most 320 MiB of HBM per device.

v0:
```python
import jax
import jax.numpy as jnp
from jax import lax
from jax.sharding import PartitionSpec as P


def contract(left, right, left_dim, right_dim):
    return lax.dot_general(
        left, right, (((left_dim,), (right_dim,)), ((), ())), preferred_element_type=jnp.float32
    )


def shards(gate_pre, up_pre, weight, block_mask, grad_out):
    block = weight.shape[0] // block_mask.shape[0]
    keep = jnp.repeat(jnp.repeat(block_mask, block, 0), block, 1).astype(jnp.bfloat16)
    masked = weight * keep
    gate32 = gate_pre.astype(jnp.float32)
    up32 = up_pre.astype(jnp.float32)
    sig = jax.nn.sigmoid(gate32)
    hidden = (gate32 * sig * up32).astype(jnp.bfloat16)
    all_hidden = lax.all_gather(hidden, "col", axis=0, tiled=True)
    all_grads = lax.all_gather(grad_out, "row", axis=0, tiled=True)
    left = all_hidden
    output = lax.psum_scatter(
        contract(left, masked, 1, 0).astype(jnp.bfloat16), "row", scatter_dimension=0, tiled=True
    )
    left = all_grads
    grad_hidden = lax.psum_scatter(
        contract(left, masked, 1, 1).astype(jnp.bfloat16), "col", scatter_dimension=0, tiled=True
    ).astype(jnp.float32)
    grad_up = (grad_hidden * gate32 * sig).astype(jnp.bfloat16)
    grad_gate = (grad_hidden * up32 * sig * (1.0 + gate32 * (1.0 - sig))).astype(jnp.bfloat16)
    product = contract(all_hidden, all_grads, 0, 0)
    grad_weight = (product * keep.astype(jnp.float32)).astype(jnp.bfloat16)
    return (output, grad_gate, grad_up, grad_weight)


def solution(mesh):
    placed = (P("col", "row"), P("col", "row"), P("row", "col"), P("row", "col"), P("row", "col"))
    return jax.shard_map(
        shards,
        mesh=mesh,
        in_specs=placed,
        out_specs=(P("row", "col"), P("col", "row"), P("col", "row"), P("row", "col")),
        check_vma=False,
    )
```

profile of v0, /device:TPU:8, one launch (start us, length us, event | category | flops | bytes accessed | tf_op | source)
XLA Modules:
  0.0 442.7 jit_solution(11824141174863572127)
XLA Ops:
  7.2 0.0 all-gather.5.cloned.1.call-start
  7.2 0.7 all-gather.5.cloned.1.call-update
  7.9 0.0 reduce-scatter.5.cloned.1.call-start
  7.9 0.7 convert_element_type.47
  8.6 103.2 %all-gather.5.cloned.1.call-done = bf16[4096,1024]{1,0:T(8,128)(2,1)} async-done(((bf16[128,1024]{1,0:T(8,128)(2,1)}), bf16[4096,1024]{1,0:T(8,128)(2,1)}) %all-gather.5.cloned.1.call-update) | async-done | bytes 8388624 | tf_op jit(solution)/shard_map/all_gather | solution.py:22
  111.8 0.6 broadcast_in_dim.7
  112.4 10.2 %fusion = bf16[4096,512]{0,1:T(8,128)(2,1)} fusion(bf16[4096,1024]{1,0:T(8,128)(2,1)} %all-gather.5.cloned.1.call-done, bf16[512,1024]{1,0:T(8,128)(2,1)} %param.7, bf16[64,8,8,128]{3,2,1,0:T(8,128)(2,1)S(1)} %bitcast.13), kind=kOutput, calls=%fused_computation.2 | convolution fusion | flops 4297588736 | bytes 14680064 | tf_op jit(solution)/shard_map/dot_general | solution.py:8
  122.7 0.0 copy-start
  122.7 0.0 copy-start.1
  122.7 0.0 reduce-scatter.5.cloned.1.call-update
  122.7 0.0 all-gather.3.cloned.1.call-start
  122.8 1.0 copy-done
  123.7 0.2 copy.9
  123.9 0.0 copy-done.1
  123.9 0.2 copy.10
  124.2 32.7 %reduce-scatter.5.cloned.1.call-done = bf16[512,512]{0,1:T(8,128)(2,1)} async-done(((bf16[4096,512]{0,1:T(8,128)(2,1)}), bf16[512,512]{0,1:T(8,128)(2,1)}) %reduce-scatter.5.cloned.1.call-update) | async-done | bytes 524304 | tf_op jit(solution)/shard_map/reduce_scatter | solution.py:28
  156.8 2.5 fusion.10
  159.3 0.0 all-gather.3.cloned.1.call-update
  159.3 0.2 reduce-scatter.3.cloned.1.call-start
  159.6 36.0 %all-gather.3.cloned.1.call-done = bf16[4096,512]{0,1:T(8,128)(2,1)} async-done(((bf16[512,512]{0,1:T(8,128)(2,1)}), bf16[4096,512]{0,1:T(8,128)(2,1)}) %all-gather.3.cloned.1.call-update) | async-done | bytes 4194320 | tf_op jit(solution)/shard_map/all_gather | solution.py:21
  195.6 10.3 %convolution_convert_fusion = bf16[4096,1024]{1,0:T(8,128)(2,1)} fusion(bf16[4096,512]{0,1:T(8,128)(2,1)} %all-gather.3.cloned.1.call-done, bf16[512,1024]{1,0:T(8,128)(2,1)} %param.7, bf16[64,8,8,128]{3,2,1,0:T(8,128)(2,1)S(1)} %bitcast.14), kind=kOutput, calls=%fused_computation | convolution fusion | flops 4299685888 | bytes 14680064 | tf_op jit(solution)/shard_map/dot_general | solution.py:8
  205.9 0.0 reduce-scatter.3.cloned.1.call-update
  205.9 1.0 copy.12
  206.9 1.0 copy.11
  207.9 10.1 %multiply_convert_fusion = bf16[512,1024]{1,0:T(8,128)(2,1)} fusion(bf16[4096,512]{0,1:T(8,128)(2,1)} %all-gather.3.cloned.1.call-done, bf16[4096,1024]{1,0:T(8,128)(2,1)} %all-gather.5.cloned.1.call-done, bf16[64,8,8,128]{3,2,1,0:T(8,128)(2,1)S(1)} %bitcast.15), kind=kOutput, calls=%fused_computation.3 | convolution fusion | flops 4296540160 | bytes 14680064 | tf_op jit(solution)/shard_map/dot_general | solution.py:8
  218.0 218.1 %reduce-scatter.3.cloned.1.call-done = bf16[128,1024]{1,0:T(8,128)(2,1)} async-done(((bf16[4096,1024]{1,0:T(8,128)(2,1)}), bf16[128,1024]{1,0:T(8,128)(2,1)}) %reduce-scatter.3.cloned.1.call-update) | async-done | bytes 262160 | tf_op jit(solution)/shard_map/reduce_scatter | solution.py:24
  (1 shorter events, 0.0 us)
Async XLA Ops:
  7.2 104.6 %all-gather.5.cloned.1.call-start = ((), (), s32[]{:S(2)}) async-start(), calls=%async_computation.4 | async-start | bytes 8650752 | tf_op jit(solution)/shard_map/all_gather | solution.py:22
  7.9 148.9 %reduce-scatter.5.cloned.1.call-start = ((), (), s32[]{:S(2)}) async-start(), calls=%async_computation.5 | async-start | bytes 4718592 | tf_op jit(solution)/shard_map/reduce_scatter | solution.py:28
  122.7 1.0 copy-start
  122.7 1.3 copy-start.1
  122.7 72.9 %all-gather.3.cloned.1.call-start = ((), (), s32[]{:S(2)}) async-start(), calls=%async_computation.2 | async-start | bytes 4718592 | tf_op jit(solution)/shard_map/all_gather | solution.py:21
  159.3 276.8 %reduce-scatter.3.cloned.1.call-start = ((), (), s32[]{:S(2)}) async-start(), calls=%async_computation.3 | async-start | bytes 8650752 | tf_op jit(solution)/shard_map/reduce_scatter | solution.py:24
Sparse Core Ops, SparseCore 0:
  10.6 101.1 all-gather.4
  122.8 33.9 reduce-scatter.4
  159.5 36.0 all-gather.2
  206.0 230.0 reduce-scatter.2
where the time goes:
time: 443 us
  waiting for transfers between devices  391 us (88%)
  matrix products  30.7 us (7%)
  between operations  13.8 us (3%)
    reduce_scatter x1, waiting for transfers between devices, shards(): lax.psum_scatter(contract(left, masked, 1, 0).astype(jnp.bfloat16), 'row'...  218 us
    all_gather x1, waiting for transfers between devices, shards(): all_grads = lax.all_gather(grad_out, 'row', axis=0, tiled=True)  103 us
    all_gather x1, waiting for transfers between devices, shards(): all_hidden = lax.all_gather(hidden, 'col', axis=0, tiled=True)  36 us
    reduce_scatter x1, waiting for transfers between devices, shards(): lax.psum_scatter(contract(left, masked, 1, 1).astype(jnp.bfloat16), 'col'...  32.7 us
    dot_general x3, matrix products, contract(): lax.dot_general(left, right, (((left_dim,), (right_dim,)), ((), ())), pre...  30.7 us
  transfers between devices with their start and end apart: 4, of which 4 were waited for; matrix products, arithmetic and copies ran while one was open for 3% of the time, Pallas kernels for 0%

commit v1 on v0

v1 whole, which is shorter than its diff:
```python
import jax
import jax.numpy as jnp
from jax import lax
from jax.experimental import pallas as pl
from jax.experimental.pallas import tpu as pltpu
from jax.sharding import PartitionSpec as P

NZ, NX, NY = 8, 4, 4
SHARD = 128
CUT = 80
REST = SHARD - CUT
MESH = pl.DeviceIdType.MESH
F32 = jnp.float32
BF16 = jnp.bfloat16
ORDER = (4, 3, -3, 2, -2, 1, -1, 0)


class Slots:
    def __init__(self):
        self.known = {}

    def __call__(self, *key):
        return self.known.setdefault(key, len(self.known))


def kernel(
    grad_ref, gate_ref, up_ref, weight_ref, mask_ref,
    out_ref, dgate_ref, dup_ref, dweight_ref,
    gall, hall, part, wm, dpart, acc,
    land_a, land_b, land_s, land_y,
    send_sem, recv_sem,
):
    row, col = lax.axis_index("row"), lax.axis_index("col")
    z, x = row // NX, row % NX
    y, core = col // 2, col % 2

    def zi(o):
        return lax.rem(z + (o + NZ), NZ)

    def xi(d):
        return lax.rem(x + (d + NX), NX)

    def yi(d):
        return lax.rem(y + (d + NY), NY)

    def zdev(d):
        return (zi(d) * NX + x, col)

    def xdev(d):
        return (z * NX + xi(d), col)

    def ydev(d):
        return (row, yi(d) * 2 + core)

    sibling = (row, y * 2 + (1 - core))

    sems, slot_a, slot_b = Slots(), Slots(), Slots()
    sends = []

    def send(src, dst, dev, *key):
        copy = pltpu.make_async_remote_copy(
            src_ref=src, dst_ref=dst, send_sem=send_sem.at[len(sends)],
            recv_sem=recv_sem.at[sems(*key)], device_id=dev, device_id_type=MESH,
        )
        copy.start()
        sends.append(copy)

    def arrive(dst, *key):
        pltpu.make_async_remote_copy(
            src_ref=dst, dst_ref=dst, send_sem=send_sem.at[0],
            recv_sem=recv_sem.at[sems(*key)], device_id=sibling, device_id_type=MESH,
        ).wait_recv()

    def add(dst, rows, *terms):
        @pl.loop(0, rows // 16)
        def _(i):
            at = pl.ds(pl.multiple_of(i * 16, 16), 16)
            total = terms[0].at[at, :][...].astype(F32)
            for term in terms[1:]:
                total = total + term.at[at, :][...].astype(F32)
            dst.at[at, :][...] = total.astype(BF16)

    barrier = pltpu.get_barrier_semaphore()
    for dev in (zdev(1), zdev(-1), xdev(1), xdev(-1), ydev(1), ydev(-1), sibling):
        pl.semaphore_signal(barrier, inc=1, device_id=dev, device_id_type=MESH)

    own_rows = pl.ds(pl.multiple_of(x * SHARD, SHARD), SHARD)

    @pl.loop(0, SHARD // 16)
    def _(i):
        at = pl.ds(pl.multiple_of(i * 16, 16), 16)
        gall[z, pl.ds(pl.multiple_of(x * SHARD + i * 16, 16), 16), :] = grad_ref[at, :]

    @pl.loop(0, 16)
    def _(i):
        at = pl.ds(pl.multiple_of(i * 32, 32), 32)
        g = gate_ref[at, :].astype(F32)
        u = up_ref[at, :].astype(F32)
        hall[col, at, :] = (g * jax.nn.sigmoid(g) * u).astype(BF16)

    pl.semaphore_wait(barrier, 7)

    def rows_a(buf, o, d):
        return buf.at[zi(o), pl.ds(pl.multiple_of(xi(d) * SHARD, 16), CUT), :]

    def rows_b(buf, o, d):
        return buf.at[zi(o), pl.ds(pl.multiple_of(xi(d) * SHARD + CUT, 16), REST), :]

    def ga(o, d):
        return rows_a(gall, o, d)

    def gb(o, d):
        return rows_b(gall, o, d)

    def hid(dy, h=None):
        at = slice(None) if h is None else pl.ds(h * 256, 256)
        return hall.at[yi(dy) * 2 + core, at, :]

    def hid_sibling(dy):
        return hall.at[yi(dy) * 2 + (1 - core)]

    def az_next(o):
        if o <= 0 and o > -4:
            send(ga(o, 0), ga(o, 0), zdev(1), "gaz", o - 1)
        if o >= 0 and o < 3:
            send(ga(o, 0), ga(o, 0), zdev(-1), "gaz", o + 1)

    def ax_first(o):
        send(ga(o, 0), ga(o, 0), xdev(1), "gax", o, -1)
        send(ga(o, 0), ga(o, 0), xdev(-1), "gax", o, 1)

    def az(o):
        arrive(ga(o, 0), "gaz", o)
        az_next(o)
        ax_first(o)

    def ax1(o):
        via = 1 if o % 2 == 0 else -1
        for d in (-via, via):
            arrive(ga(o, d), "gax", o, d)
            if d == -via:
                send(ga(o, d), ga(o, d), xdev(via), "gax", o, 2)

    def ax2(o):
        arrive(ga(o, 2), "gax", o, 2)

    def bz_first(d):
        send(gb(0, d), gb(0, d), zdev(1), "gbz", d, -1)
        send(gb(0, d), gb(0, d), zdev(-1), "gbz", d, 1)

    def bx(d):
        arrive(gb(0, d), "gbx", d)
        if d == -1:
            send(gb(0, d), gb(0, d), xdev(1), "gbx", 2)
        bz_first(d)

    def bz(o, d):
        low, high = (-4, 3) if d % 2 == 0 else (-3, 4)
        if o < low or o > high:
            return
        arrive(gb(o, d), "gbz", d, o)
        if o < 0 and o > low:
            send(gb(o, d), gb(o, d), zdev(1), "gbz", d, o - 1)
        if o > 0 and o < high:
            send(gb(o, d), gb(o, d), zdev(-1), "gbz", d, o + 1)

    def bz_all(k):
        for d in (0, -1, 1, 2):
            bz(-k, d)
            bz(k, d)

    def h0():
        for h in (0, 1):
            send(hid(0, h), hid(0, h), ydev(1), "hy", -1, h)
            send(hid(0, 1 - h), hid(0, 1 - h), ydev(-1), "hy", 1, 1 - h)
        send(hid(0), hid(0), sibling, "hs", 0)

    def h1():
        arrive(hid(-1, 0), "hy", -1, 0)
        send(hid(-1, 0), hid(-1, 0), ydev(1), "hy2", 0)
        arrive(hid(1, 1), "hy", 1, 1)
        send(hid(1, 1), hid(1, 1), ydev(-1), "hy2", 1)

    def h2():
        arrive(hid(-1, 1), "hy", -1, 1)
        send(hid(-1), hid(-1), sibling, "hs", -1)
        arrive(hid(1, 0), "hy", 1, 0)
        send(hid(1), hid(1), sibling, "hs", 1)

    def h3():
        arrive(hid(2, 0), "hy2", 0)
        arrive(hid(2, 1), "hy2", 1)
        send(hid(2), hid(2), sibling, "hs", 2)

    def h4():
        for dy in (0, -1, 1, 2):
            arrive(hid_sibling(dy), "hs", dy)

    def mm_part(o):
        block = zi(o)

        @pl.loop(0, 4)
        def _(n):
            at = pl.ds(pl.multiple_of(n * 256, 256), 256)
            part[block, :, at] = jnp.dot(hall[block], wm[:, at], preferred_element_type=F32).astype(BF16)

    def mm_dpart(block):
        @pl.loop(0, 2)
        def _(n):
            at = pl.ds(pl.multiple_of(n * 256, 256), 256)
            dpart[block, :, at] = lax.dot_general(
                gall[block], wm[at, :], (((1,), (1,)), ((), ())), preferred_element_type=F32
            ).astype(BF16)

    def mm_weight(block, first):
        @pl.loop(0, 4)
        def _(n):
            at = pl.ds(pl.multiple_of(n * 256, 256), 256)
            product = lax.dot_general(
                hall[block], gall[block, :, at], (((0,), (0,)), ((), ())), preferred_element_type=F32
            )
            acc[:, at] = product if first else acc[:, at] + product

    def pa(o, d):
        return rows_a(part, o, d)

    def pb(o, d):
        return rows_b(part, o, d)

    def la(*key):
        return land_a.at[slot_a(*key)]

    def lb(*key):
        return land_b.at[slot_b(*key)]

    def via_of(o):
        return 1 if o % 2 == 0 else -1

    def xs(o):
        via = via_of(o)
        send(pa(o, 2), la("pxm", o), xdev(via), "pxm", o)
        send(pa(o, -via), la("pxl", o, via), xdev(-via), "pxl", o, via)

    def xm(o):
        via = via_of(o)
        held = la("pxm", o)
        arrive(held, "pxm", o)
        add(held, CUT, held, pa(o, via))
        send(held, la("pxl", o, -via), xdev(via), "pxl", o, -via)

    def zf(o):
        sides = []
        if 0 <= o < 4:
            sides.append(-1)
        if -3 < o <= 0:
            sides.append(1)
        left, right = la("pxl", o, -1), la("pxl", o, 1)
        arrive(left, "pxl", o, -1)
        arrive(right, "pxl", o, 1)
        terms = [pa(o, 0), left, right]
        for side in sides:
            held = la("pz", o, side)
            arrive(held, "pz", o, side)
            terms.append(held)
        if o == 0:
            add(out_ref.at[pl.ds(0, CUT), :], CUT, *terms)
            return
        add(left, CUT, *terms)
        if o > 0:
            send(left, la("pz", o - 1, -1), zdev(1), "pz", o - 1, -1)
        else:
            send(left, la("pz", o + 1, 1), zdev(-1), "pz", o + 1, 1)

    def rz(o):
        for d in (0, -1, 1, 2):
            even = d % 2 == 0
            sides = []
            if 0 <= o < 4 and not (o == 3 and not even):
                sides.append(-1)
            if -4 < o <= 0 and not (o == -3 and even):
                sides.append(1)
            terms = [pb(o, d)]
            for side in sides:
                held = lb("pbz", d, o, side)
                arrive(held, "pbz", d, o, side)
                terms.append(held)
            src = terms[-1]
            if len(terms) > 1:
                add(src, REST, *terms)
            if o == 4:
                if even:
                    send(src, lb("pbz", d, 3, -1), zdev(1), "pbz", d, 3, -1)
                else:
                    send(src, lb("pbz", d, -3, 1), zdev(-1), "pbz", d, -3, 1)
            elif o > 0:
                send(src, lb("pbz", d, o - 1, -1), zdev(1), "pbz", d, o - 1, -1)
            elif o < 0:
                send(src, lb("pbz", d, o + 1, 1), zdev(-1), "pbz", d, o + 1, 1)

    def rsum(d):
        return lb("pbz", d, 0, 1)

    def bs():
        send(rsum(2), lb("pbxm"), xdev(1), "pbxm")
        send(rsum(-1), lb("pbxl", 1), xdev(-1), "pbxl", 1)

    def bm():
        held = lb("pbxm")
        arrive(held, "pbxm")
        add(held, REST, held, rsum(1))
        send(held, lb("pbxl", -1), xdev(1), "pbxl", -1)

    def bf():
        left, right = lb("pbxl", -1), lb("pbxl", 1)
        arrive(left, "pbxl", -1)
        arrive(right, "pbxl", 1)
        add(out_ref.at[pl.ds(CUT, REST), :], REST, rsum(0), left, right)

    def own(dy):
        return yi(dy) * 2 + core

    def dhalf(dy, h):
        return dpart.at[own(dy), pl.ds(h * 256, 256), :]

    S = {2: 0, -1: 1, 1: 2, 0: 3}
    Y = {("m", -1): 0, ("m", 1): 1, (-1, 0): 2, (-1, 1): 3, (1, 0): 4, (1, 1): 5}

    def ly(*key):
        return land_y.at[Y[key]]

    def ds_(dy):
        other = yi(dy) * 2 + (1 - core)
        mm_dpart(other)
        send(dpart.at[other], land_s.at[S[dy]], sibling, "ds", dy)
        mm_dpart(own(dy))

    def da(dy):
        held = land_s.at[S[dy]]
        arrive(held, "ds", dy)
        mine = dpart.at[own(dy)]
        add(mine, 512, mine, held)
        if dy == 2:
            send(dhalf(2, 0), ly("m", -1), ydev(1), "dym", -1)
            send(dhalf(2, 1), ly("m", 1), ydev(-1), "dym", 1)
        if dy == 1:
            send(dhalf(1, 1), ly(-1, 1), ydev(1), "dyf", -1, 1)
        if dy == -1:
            send(dhalf(-1, 0), ly(1, 0), ydev(-1), "dyf", 1, 0)

    def dm():
        for side, h in ((-1, 0), (1, 1)):
            held = ly("m", side)
            arrive(held, "dym", side)
            add(held, 256, held, dhalf(-side, h))
            send(held, ly(side, h), ydev(-side), "dyf", side, h)

    def df():
        for h in (1, 0):
            for side in (-1, 1):
                arrive(ly(side, h), "dyf", side, h)
        for h in (0, 1):
            @pl.loop(0, 8)
            def _(i):
                at = pl.ds(pl.multiple_of(i * 32, 32), 32)
                rows = pl.ds(pl.multiple_of(h * 256 + i * 32, 32), 32)
                dh = (
                    dhalf(0, h).at[at, :][...].astype(F32)
                    + ly(-1, h).at[at, :][...].astype(F32)
                    + ly(1, h).at[at, :][...].astype(F32)
                )
                g = gate_ref[rows, :].astype(F32)
                u = up_ref[rows, :].astype(F32)
                sig = jax.nn.sigmoid(g)
                dup_ref[rows, :] = (dh * g * sig).astype(BF16)
                dgate_ref[rows, :] = (dh * u * sig * (1.0 + g * (1.0 - sig))).astype(BF16)

    def mask_into(dst, src):
        @pl.loop(0, 4)
        def _(i):
            at = pl.ds(pl.multiple_of(i * 128, 128), 128)
            for j in range(8):
                cols = pl.ds(j * 128, 128)
                dst[at, cols] = (src[at, cols].astype(F32) * mask_ref[i, j].astype(F32)).astype(BF16)

    send(gb(0, 0), gb(0, 0), xdev(1), "gbx", -1)
    send(gb(0, 0), gb(0, 0), xdev(-1), "gbx", 1)
    az_next(0)
    ax_first(0)
    bz_first(0)
    h0()
    mask_into(wm, weight_ref)
    bx(-1)
    bx(1)
    az(-1)
    az(1)
    ax1(0)
    bx(2)
    h1()
    bz_all(1)
    az(-2)
    az(2)
    ax1(-1)
    ax1(1)
    h2()
    bz_all(2)
    h3()
    az(-3)
    az(3)
    ax1(-2)
    ax1(2)
    h4()
    mm_part(ORDER[0])
    bz_all(3)
    mm_part(ORDER[1])
    az(-4)
    ax1(-3)
    ax1(3)
    mm_part(ORDER[2])
    xs(ORDER[0])
    rz(ORDER[0])
    bz_all(4)
    mm_part(ORDER[3])
    ax1(-4)
    xs(ORDER[1])
    for o in (0, -1, 1, -2, 2, -3, 3, -4):
        ax2(o)

    def tick(t):
        if t + 1 < 8 and t >= 1:
            xs(ORDER[t + 1])
        if 1 <= t <= 8:
            xm(ORDER[t - 1])
        if 1 <= t <= 7:
            rz(ORDER[t])
        if 2 <= t <= 9:
            zf(ORDER[t - 2])
        if t + 4 < 8:
            mm_part(ORDER[t + 4])
        if t == 7:
            bs()
        if t == 8:
            bm()
        if t == 9:
            bf()

    def weight_piece(k):
        mm_weight(k, k == 0)

    tick(0)
    ds_(2)
    tick(1)
    ds_(-1)
    da(2)
    tick(2)
    ds_(1)
    da(-1)
    tick(3)
    ds_(0)
    da(1)
    tick(4)
    dm()
    da(0)
    weight_piece(0)
    tick(5)
    weight_piece(1)
    weight_piece(2)
    tick(6)
    weight_piece(3)
    weight_piece(4)
    tick(7)
    df()
    weight_piece(5)
    tick(8)
    weight_piece(6)
    weight_piece(7)
    mask_into(dweight_ref, acc)
    tick(9)

    for copy in sends:
        copy.wait_send()


def shards(gate_pre, up_pre, weight, block_mask, grad_out):
    vmem = pl.BlockSpec(memory_space=pltpu.VMEM)
    return pl.pallas_call(
        kernel,
        out_shape=(
            jax.ShapeDtypeStruct((SHARD, 1024), BF16),
            jax.ShapeDtypeStruct((512, 512), BF16),
            jax.ShapeDtypeStruct((512, 512), BF16),
            jax.ShapeDtypeStruct((512, 1024), BF16),
        ),
        in_specs=[vmem] * 4 + [pl.BlockSpec(memory_space=pltpu.SMEM)],
        out_specs=[vmem] * 4,
        scratch_shapes=[
            pltpu.VMEM((NZ, 512, 1024), BF16),
            pltpu.VMEM((8, 512, 512), BF16),
            pltpu.VMEM((NZ, 512, 1024), BF16),
            pltpu.VMEM((512, 1024), BF16),
            pltpu.VMEM((8, 512, 512), BF16),
            pltpu.VMEM((512, 1024), F32),
            pltpu.VMEM((31, CUT, 1024), BF16),
            pltpu.VMEM((31, REST, 1024), BF16),
            pltpu.VMEM((4, 512, 512), BF16),
            pltpu.VMEM((6, 256, 512), BF16),
            pltpu.SemaphoreType.DMA((144,)),
            pltpu.SemaphoreType.DMA((144,)),
        ],
        compiler_params=pltpu.CompilerParams(
            collective_id=0, has_side_effects=True, vmem_limit_bytes=58 * 2**20
        ),
        cost_estimate=pl.CostEstimate(flops=12 * 2**30, bytes_accessed=8 * 2**20, transcendentals=2**19),
    )(grad_out, gate_pre, up_pre, weight, block_mask)


def solution(mesh):
    placed = (P("col", "row"), P("col", "row"), P("row", "col"), P("row", "col"), P("row", "col"))
    return jax.shard_map(
        shards,
        mesh=mesh,
        in_specs=placed,
        out_specs=(P("row", "col"), P("col", "row"), P("col", "row"), P("row", "col")),
        check_vma=False,
    )
```

time: 443 us -> 124 us (0.28)
  waiting for transfers between devices: 391 us -> 0 us
  Pallas kernels: 0 us -> 119 us
  matrix products: 30.7 us -> 0 us
  between operations: 13.8 us -> 0.66 us
    reduce_scatter x2 -> x0, waiting for transfers between devices: 251 us -> none  [the longest x1 218 us: shards(): lax.psum_scatter(contract(left, masked, 1, 0).astype(jnp.bfloat16), 'row'...]
    all_gather x2 -> x0, waiting for transfers between devices: 139 us -> none  [the longest x1 103 us: shards(): all_grads = lax.all_gather(grad_out, 'row', axis=0, tiled=True)]
    pallas_call x0 -> x1, Pallas kernels: none -> 119 us  [shards(): pl.pallas_call(kernel, out_shape=(jax.ShapeDtypeStruct((SHARD, 1024), BF1...]
    dot_general x3 -> x0, matrix products: 30.7 us -> none  [contract(): lax.dot_general(left, right, (((left_dim,), (right_dim,)), ((), ())), pre...]
  transfers between devices with their start and end apart: 4 -> 0, of which waited for: 4 -> 0; matrix products, arithmetic and copies ran while one was open for 3% -> 0% of each run, Pallas kernels for 0% -> 0%
where the time goes in v1:
time: 124 us
  Pallas kernels  119 us (96%)
  local copies, waits for them, and re-layouts  4.32 us (3%)
    pallas_call x1, Pallas kernels, shards(): pl.pallas_call(kernel, out_shape=(jax.ShapeDtypeStruct((SHARD, 1024), BF1...  119 us
    unnamed x10, local copies, waits for them, and re-layouts  4.32 us

profile of v1, /device:TPU:8, one launch (start us, length us, event | category | flops | bytes accessed | tf_op | source)
XLA Modules:
  0.0 123.9 jit_solution(10575315236843610203)
XLA Ops:
  0.6 118.9 %shard_map.84 = (bf16[128,1024]{1,0:T(8,128)(2,1)}, bf16[512,512]{1,0:T(8,128)(2,1)}, bf16[512,512]{1,0:T(8,128)(2,1)}, bf16[512,1024]{1,0:T(8,128)(2,1)}) custom-call(bf16[128,1024]{1,0:T(8,128)(2,1)} %grad_ref.1, bf16[512,512]{1,0:T(8,128)(2,1)} %gate_ref.1, bf16[512,512]{1,0:T(8,128)(2,1)} %up_ref.1, bf16[512,1024]{1,0:T(8,128)(2,1)} %weight_ref.1, ...), custom_call_target="tpu_custom_call" | custom-call | flops 12884901888 | bytes 8388608 | tf_op jit(solution)/shard_map/pallas_call | solution.py:485
  119.6 0.0 copy-start.2
  119.6 0.0 copy-start.1
  119.6 1.8 %copy.13 = bf16[128,1024]{1,0:T(8,128)(2,1)} copy(bf16[128,1024]{1,0:T(8,128)(2,1)} %get-tuple-element.8) | data formatting | bytes 524288
  121.3 0.0 copy-done.2
  121.3 0.0 copy-start
  121.3 0.8 copy.14
  122.1 0.0 copy-done.1
  122.1 0.8 copy.15
  122.9 0.0 copy-done
  122.9 1.0 copy.16
Async XLA Ops:
  119.6 1.8 %copy-start.2 = (bf16[512,512]{1,0:T(8,128)(2,1)S(1)}, bf16[512,512]{1,0:T(8,128)(2,1)}, u32[]{:S(2)}) copy-start(bf16[512,512]{1,0:T(8,128)(2,1)} %get-tuple-element.9) | copy-start | bytes 1572868
  119.6 2.6 %copy-start.1 = (bf16[512,512]{1,0:T(8,128)(2,1)S(1)}, bf16[512,512]{1,0:T(8,128)(2,1)}, u32[]{:S(2)}) copy-start(bf16[512,512]{1,0:T(8,128)(2,1)} %get-tuple-element.10) | copy-start | bytes 1572868
  121.3 1.6 %copy-start = (bf16[512,1024]{1,0:T(8,128)(2,1)S(1)}, bf16[512,1024]{1,0:T(8,128)(2,1)}, u32[]{:S(2)}) copy-start(bf16[512,1024]{1,0:T(8,128)(2,1)} %get-tuple-element.11) | copy-start | bytes 3145732

commit v2 on v0

v2 whole, which is shorter than its diff:
```python
import jax
import jax.numpy as jnp
from jax import lax
from jax.experimental import pallas as pl
from jax.experimental.pallas import tpu as pltpu
from jax.sharding import PartitionSpec as P

NZ, NX, NY = 8, 4, 4
SHARD = 128
CUT = 32
REST = SHARD - CUT
MESH = pl.DeviceIdType.MESH
F32 = jnp.float32
BF16 = jnp.bfloat16
ORDER = (4, 3, -3, 2, -2, 1, -1, 0)


class Slots:
    def __init__(self):
        self.known = {}

    def __call__(self, *key):
        return self.known.setdefault(key, len(self.known))


def dot(a, b, a_dim, b_dim):
    return lax.dot_general(a, b, (((a_dim,), (b_dim,)), ((), ())), preferred_element_type=F32)


def tile(n, size):
    return pl.ds(pl.multiple_of(n * size, size), size)


def kernel(
    grad_ref, gate_ref, up_ref, weight_ref, mask_ref,
    out_ref, dgate_ref, dup_ref, dweight_ref,
    gall, hall, hx, part, wm, wo, dpart, acc, accx, wsend, wrecv,
    land_a, land_b, land_s, land_y, land_x,
    send_sem, recv_sem,
):
    row, col = lax.axis_index("row"), lax.axis_index("col")
    z, x = row // NX, row % NX
    y, core = col // 2, col % 2
    parity = x % 2
    near = 1 - 2 * parity

    def zi(o):
        return lax.rem(z + (o + NZ), NZ)

    def xi(d):
        return lax.rem(x + (d + NX), NX)

    def yi(d):
        return lax.rem(y + (d + NY), NY)

    def zdev(d):
        return (zi(d) * NX + x, col)

    def xdev(d):
        return (z * NX + xi(d), col)

    def ydev(d):
        return (row, yi(d) * 2 + core)

    sibling = (row, y * 2 + (1 - core))
    mates = (xdev(near), xdev(-near))
    across = xdev(2)

    sems, slot_a, slot_b = Slots(), Slots(), Slots()
    sends = []

    def send(src, dst, dev, *key):
        copy = pltpu.make_async_remote_copy(
            src_ref=src, dst_ref=dst, send_sem=send_sem.at[len(sends)],
            recv_sem=recv_sem.at[sems(*key)], device_id=dev, device_id_type=MESH,
        )
        copy.start()
        sends.append(copy)

    def arrive(dst, *key):
        pltpu.make_async_remote_copy(
            src_ref=dst, dst_ref=dst, send_sem=send_sem.at[0],
            recv_sem=recv_sem.at[sems(*key)], device_id=sibling, device_id_type=MESH,
        ).wait_recv()

    def add(dst, rows, *terms):
        @pl.loop(0, rows // 16)
        def _(i):
            at = tile(i, 16)
            total = terms[0].at[at, :][...].astype(F32)
            for term in terms[1:]:
                total = total + term.at[at, :][...].astype(F32)
            dst.at[at, :][...] = total.astype(BF16)

    barrier = pltpu.get_barrier_semaphore()
    for dev in (zdev(1), zdev(-1), xdev(1), xdev(-1), across, ydev(1), ydev(-1), sibling):
        pl.semaphore_signal(barrier, inc=1, device_id=dev, device_id_type=MESH)

    mine, other = x // 2, 1 - x // 2

    @pl.loop(0, SHARD // 16)
    def _(i):
        gall[z, pl.ds(pl.multiple_of(mine * SHARD + i * 16, 16), 16), :] = grad_ref[tile(i, 16), :]

    def hidden_into(dst, which):
        for j in (0, 1):
            @pl.loop(0, 4)
            def _(i):
                at = pl.ds(pl.multiple_of((which + 2 * j) * SHARD + i * 32, 32), 32)
                g = gate_ref[at, :].astype(F32)
                u = up_ref[at, :].astype(F32)
                dst.at[pl.ds(pl.multiple_of(j * SHARD + i * 32, 32), 32), :][...] = (
                    g * jax.nn.sigmoid(g) * u
                ).astype(BF16)

    hidden_into(hx, 1 - parity)
    hidden_into(hall.at[0, col], parity)

    pl.semaphore_wait(barrier, 8)

    def rows_a(buf, o, e):
        return buf.at[zi(o), pl.ds(pl.multiple_of((other if e else mine) * SHARD, 16), CUT), :]

    def rows_b(buf, o, e):
        return buf.at[zi(o), pl.ds(pl.multiple_of((other if e else mine) * SHARD + CUT, 16), REST), :]

    def ga(o, e):
        return rows_a(gall, o, e)

    def gb(o, e):
        return rows_b(gall, o, e)

    def hid(f, dy, h=None):
        at = slice(None) if h is None else pl.ds(h * 128, 128)
        return hall.at[f, yi(dy) * 2 + core, at, :]

    def hid_sibling(f, dy):
        return hall.at[f, yi(dy) * 2 + (1 - core)]

    def az_next(o):
        if o <= 0 and o > -4:
            send(ga(o, 0), ga(o, 0), zdev(1), "gaz", o - 1)
        if o >= 0 and o < 3:
            send(ga(o, 0), ga(o, 0), zdev(-1), "gaz", o + 1)

    def ax_send(o):
        send(ga(o, 0), ga(o, 0), across, "gax", o)

    def az(*offsets):
        for o in offsets:
            arrive(ga(o, 0), "gaz", o)
            az_next(o)
            ax_send(o)

    def ax(*offsets):
        for o in offsets:
            arrive(ga(o, 1), "gax", o)

    def bz_first(e):
        send(gb(0, e), gb(0, e), zdev(1), "gbz", e, -1)
        send(gb(0, e), gb(0, e), zdev(-1), "gbz", e, 1)

    def bx():
        arrive(gb(0, 1), "gbx")
        bz_first(1)

    def bz(k, e):
        low, high = (-4, 3) if e == 0 else (-3, 4)
        for o in (-k, k):
            if o < low or o > high:
                continue
            arrive(gb(o, e), "gbz", e, o)
            if o < 0 and o > low:
                send(gb(o, e), gb(o, e), zdev(1), "gbz", e, o - 1)
            if o > 0 and o < high:
                send(gb(o, e), gb(o, e), zdev(-1), "gbz", e, o + 1)

    def h0(f):
        for h in (0, 1):
            send(hid(f, 0, h), hid(f, 0, h), ydev(1), "hy", f, -1, h)
            send(hid(f, 0, 1 - h), hid(f, 0, 1 - h), ydev(-1), "hy", f, 1, 1 - h)
        send(hid(f, 0), hid(f, 0), sibling, "hs", f, 0)

    def h1(f):
        arrive(hid(f, -1, 0), "hy", f, -1, 0)
        send(hid(f, -1, 0), hid(f, -1, 0), ydev(1), "hy2", f, 0)
        arrive(hid(f, 1, 1), "hy", f, 1, 1)
        send(hid(f, 1, 1), hid(f, 1, 1), ydev(-1), "hy2", f, 1)

    def h2(f):
        arrive(hid(f, -1, 1), "hy", f, -1, 1)
        send(hid(f, -1), hid(f, -1), sibling, "hs", f, -1)
        arrive(hid(f, 1, 0), "hy", f, 1, 0)
        send(hid(f, 1), hid(f, 1), sibling, "hs", f, 1)

    def h3(f):
        arrive(hid(f, 2, 0), "hy2", f, 0)
        arrive(hid(f, 2, 1), "hy2", f, 1)
        send(hid(f, 2), hid(f, 2), sibling, "hs", f, 2)

    def h4(f):
        for dy in (0, -1, 1, 2):
            arrive(hid_sibling(f, dy), "hs", f, dy)

    def mm_part(o):
        block = zi(o)
        for s in (0, 1):
            @pl.loop(0, 2)
            def _(n):
                at = tile(n, 256)
                part[block, :, pl.ds(pl.multiple_of(s * 512 + n * 256, 256), 256)] = (
                    dot(hall[0, block], wm[s, :, at], 1, 0) + dot(hall[1 + s, block], wo[s, :, at], 1, 0)
                ).astype(BF16)

    def mm_dpart(block):
        @pl.loop(0, 2)
        def _(n):
            at = tile(n, 256)
            first, second = gall[block, :, pl.ds(0, 512)], gall[block, :, pl.ds(512, 512)]
            dpart[1, block, :, at] = dot(first, wo[0, at, :], 1, 1).astype(BF16)
            dpart[2, block, :, at] = dot(second, wo[1, at, :], 1, 1).astype(BF16)
            dpart[0, block, :, at] = (dot(first, wm[0, at, :], 1, 1) + dot(second, wm[1, at, :], 1, 1)).astype(BF16)

    def mm_weight(k):
        pair = pl.ds(2 * k, 2)

        def gsum(dst, at, f, cols):
            product = dot(
                hall[f, pair].reshape(512, 512), gall[pair, :, cols].reshape(512, 256), 0, 0
            )
            dst[:, at] = product if k == 0 else dst[:, at] + product

        for s in (0, 1):
            @pl.loop(0, 2)
            def _(n):
                gsum(accx.at[s], tile(n, 256), 1 + s, pl.ds(pl.multiple_of(s * 512 + n * 256, 256), 256))

        @pl.loop(0, 4)
        def _(n):
            gsum(acc, tile(n, 256), 0, tile(n, 256))

    def pa(o, e):
        return rows_a(part, o, e)

    def pb(o, e):
        return rows_b(part, o, e)

    def la(*key):
        return land_a.at[slot_a(*key)]

    def lb(*key):
        return land_b.at[slot_b(*key)]

    def xs(o):
        send(pa(o, 1), la("px", o), across, "px", o)

    def zf(o):
        sides = []
        if 0 <= o < 4:
            sides.append(-1)
        if -3 < o <= 0:
            sides.append(1)
        held = la("px", o)
        arrive(held, "px", o)
        terms = [pa(o, 0), held]
        for side in sides:
            arrive(la("pz", o, side), "pz", o, side)
            terms.append(la("pz", o, side))
        if o == 0:
            add(out_ref.at[pl.ds(0, CUT), :], CUT, *terms)
            return
        add(held, CUT, *terms)
        if o > 0:
            send(held, la("pz", o - 1, -1), zdev(1), "pz", o - 1, -1)
        else:
            send(held, la("pz", o + 1, 1), zdev(-1), "pz", o + 1, 1)

    def rz(o):
        for e in (1, 0):
            sides = []
            if 0 <= o < 4 and not (o == 3 and e == 1):
                sides.append(-1)
            if -4 < o <= 0 and not (o == -3 and e == 0):
                sides.append(1)
            terms = [pb(o, e)]
            for side in sides:
                held = lb("pbz", e, o, side)
                arrive(held, "pbz", e, o, side)
                terms.append(held)
            src = terms[-1]
            if len(terms) > 1:
                add(src, REST, *terms)
            if o == 4:
                if e == 0:
                    send(src, lb("pbz", e, 3, -1), zdev(1), "pbz", e, 3, -1)
                else:
                    send(src, lb("pbz", e, -3, 1), zdev(-1), "pbz", e, -3, 1)
            elif o > 0:
                send(src, lb("pbz", e, o - 1, -1), zdev(1), "pbz", e, o - 1, -1)
            elif o < 0:
                send(src, lb("pbz", e, o + 1, 1), zdev(-1), "pbz", e, o + 1, 1)
            elif e == 1:
                send(src, lb("pbx"), across, "pbx")

    def bf():
        held = lb("pbx")
        arrive(held, "pbx")
        add(out_ref.at[pl.ds(CUT, REST), :], REST, lb("pbz", 0, 0, 1), held)

    S = {2: 0, -1: 1, 1: 2, 0: 3}
    Y = {("m", -1): 0, ("m", 1): 1, (-1, 0): 2, (-1, 1): 3, (1, 0): 4, (1, 1): 5}
    FS = (1, 2, 0)

    def own(dy):
        return yi(dy) * 2 + core

    def dhalf(f, dy, h):
        return dpart.at[f, own(dy), pl.ds(h * 128, 128), :]

    def ly(f, *key):
        return land_y.at[f, Y[key]]

    def dsib(dy):
        block = yi(dy) * 2 + (1 - core)
        mm_dpart(block)
        for f in FS:
            send(dpart.at[f, block], land_s.at[f, S[dy]], sibling, "ds", f, dy)
        mm_dpart(own(dy))

    def dadd(dy):
        for f in FS:
            held = land_s.at[f, S[dy]]
            arrive(held, "ds", f, dy)
            here = dpart.at[f, own(dy)]
            add(here, 256, here, held)
            if dy == 2:
                send(dhalf(f, 2, 0), ly(f, "m", -1), ydev(1), "dym", f, -1)
                send(dhalf(f, 2, 1), ly(f, "m", 1), ydev(-1), "dym", f, 1)
            if dy == 1:
                send(dhalf(f, 1, 1), ly(f, -1, 1), ydev(1), "dyf", f, -1, 1)
            if dy == -1:
                send(dhalf(f, -1, 0), ly(f, 1, 0), ydev(-1), "dyf", f, 1, 0)

    def dmid(f):
        for side, h in ((-1, 0), (1, 1)):
            held = ly(f, "m", side)
            arrive(held, "dym", f, side)
            add(held, 128, held, dhalf(f, -side, h))
            send(held, ly(f, side, h), ydev(-side), "dyf", f, side, h)

    def dend(f):
        for h in (1, 0):
            for side in (-1, 1):
                arrive(ly(f, side, h), "dyf", f, side, h)

    def dmate(f):
        dend(f)
        for h in (0, 1):
            add(dhalf(f, 0, h), 128, dhalf(f, 0, h), ly(f, -1, h), ly(f, 1, h))
        send(dpart.at[f, own(0)], land_x.at[f - 1], mates[f - 1], "dx", f)

    def grads(which, j, *terms):
        @pl.loop(0, 4)
        def _(i):
            at = tile(i, 32)
            rows = pl.ds(pl.multiple_of((which + 2 * j) * SHARD + i * 32, 32), 32)
            dh = terms[0].at[at, :][...].astype(F32)
            for term in terms[1:]:
                dh = dh + term.at[at, :][...].astype(F32)
            g = gate_ref[rows, :].astype(F32)
            u = up_ref[rows, :].astype(F32)
            sig = jax.nn.sigmoid(g)
            dup_ref[rows, :] = (dh * g * sig).astype(BF16)
            dgate_ref[rows, :] = (dh * u * sig * (1.0 + g * (1.0 - sig))).astype(BF16)

    def grads_own():
        dend(0)
        for h in (0, 1):
            grads(parity, h, dhalf(0, 0, h), ly(0, -1, h), ly(0, 1, h))

    def grads_mates():
        for f in (1, 2):
            arrive(land_x.at[f - 1], "dx", f)
        for h in (0, 1):
            at = pl.ds(h * 128, 128)
            grads(1 - parity, h, land_x.at[0, at, :], land_x.at[1, at, :])

    def keep(i, j):
        return mask_ref[i, j].astype(F32)

    def mask_weights():
        @pl.loop(0, 4)
        def _(i):
            for j in range(8):
                wm[j // 4, tile(i, 128), pl.ds(j % 4 * 128, 128)] = (
                    weight_ref[tile(i, 128), pl.ds(j * 128, 128)].astype(F32) * keep(i, j)
                ).astype(BF16)

    def weights_out():
        for s in (0, 1):
            send(wm.at[s], wo.at[s], mates[s], "w", s)

    def weights_in():
        for s in (0, 1):
            arrive(wo.at[s], "w", s)

    def dweights_out():
        for s in (0, 1):
            @pl.loop(0, 16)
            def _(i):
                wsend[s, tile(i, 32), :] = accx[s, tile(i, 32), :].astype(BF16)
            send(wsend.at[s], wrecv.at[s], mates[s], "dw", s)

    def dweights_in():
        for s in (0, 1):
            arrive(wrecv.at[s], "dw", s)

        @pl.loop(0, 4)
        def _(i):
            for j in range(8):
                cols = pl.ds(j * 128, 128)
                total = acc[tile(i, 128), cols] + wrecv[j // 4, tile(i, 128), pl.ds(j % 4 * 128, 128)].astype(F32)
                dweight_ref[tile(i, 128), cols] = (total * keep(i, j)).astype(BF16)

    bz_first(0)
    az_next(0)
    for s in (0, 1):
        send(hx, hall.at[1 + s, col], mates[s], "hx", s)
    send(gb(0, 0), gb(0, 0), across, "gbx")
    h0(0)
    ax_send(0)
    mask_weights()
    h1(0)
    bz(1, 0)
    for s in (0, 1):
        arrive(hall.at[1 + s, col], "hx", s)
    h0(1)
    h0(2)
    az(-1, 1)
    h2(0)
    h3(0)
    bx()
    weights_out()
    bz(2, 0)
    h1(1)
    bz(1, 1)
    h2(1)
    az(-2, 2)
    h3(1)
    bz(3, 0)
    h1(2)
    h2(2)
    bz(2, 1)
    az(-3, 3)
    h3(2)
    weights_in()
    for f in (0, 1, 2):
        h4(f)
    mm_part(ORDER[0])
    bz(4, 0)
    mm_part(ORDER[1])
    bz(3, 1)
    mm_part(ORDER[2])
    xs(ORDER[0])
    rz(ORDER[0])
    az(-4)
    bz(4, 1)
    mm_part(ORDER[3])
    xs(ORDER[1])
    ax(0, -1, 1, -2, 2, -3, 3, -4)

    def tick(t):
        if 1 <= t < 7:
            xs(ORDER[t + 1])
        if 1 <= t <= 7:
            rz(ORDER[t])
        if 1 <= t <= 8:
            zf(ORDER[t - 1])
        if t + 3 < 8 and t >= 1:
            mm_part(ORDER[t + 3])

    dsib(2)
    tick(1)
    dsib(-1)
    dadd(2)
    tick(2)
    dsib(1)
    dadd(-1)
    tick(3)
    dadd(1)
    dmid(1)
    dsib(0)
    tick(4)
    dmid(2)
    dadd(0)
    dmid(0)
    mm_weight(0)
    mm_weight(1)
    tick(5)
    mm_weight(2)
    mm_weight(3)
    dweights_out()
    dmate(1)
    tick(6)
    dmate(2)
    tick(7)
    grads_own()
    dweights_in()
    grads_mates()
    tick(8)
    bf()

    for copy in sends:
        copy.wait_send()


def shards(gate_pre, up_pre, weight, block_mask, grad_out):
    vmem = pl.BlockSpec(memory_space=pltpu.VMEM)
    return pl.pallas_call(
        kernel,
        out_shape=(
            jax.ShapeDtypeStruct((SHARD, 1024), BF16),
            jax.ShapeDtypeStruct((512, 512), BF16),
            jax.ShapeDtypeStruct((512, 512), BF16),
            jax.ShapeDtypeStruct((512, 1024), BF16),
        ),
        in_specs=[vmem] * 4 + [pl.BlockSpec(memory_space=pltpu.SMEM)],
        out_specs=[vmem] * 4,
        scratch_shapes=[
            pltpu.VMEM((NZ, 256, 1024), BF16),
            pltpu.VMEM((3, 8, 256, 512), BF16),
            pltpu.VMEM((256, 512), BF16),
            pltpu.VMEM((NZ, 256, 1024), BF16),
            pltpu.VMEM((2, 512, 512), BF16),
            pltpu.VMEM((2, 512, 512), BF16),
            pltpu.VMEM((3, 8, 256, 512), BF16),
            pltpu.VMEM((512, 1024), F32),
            pltpu.VMEM((2, 512, 512), F32),
            pltpu.VMEM((2, 512, 512), BF16),
            pltpu.VMEM((2, 512, 512), BF16),
            pltpu.VMEM((15, CUT, 1024), BF16),
            pltpu.VMEM((15, REST, 1024), BF16),
            pltpu.VMEM((3, 4, 256, 512), BF16),
            pltpu.VMEM((3, 6, 128, 512), BF16),
            pltpu.VMEM((2, 256, 512), BF16),
            pltpu.SemaphoreType.DMA((128,)),
            pltpu.SemaphoreType.DMA((128,)),
        ],
        compiler_params=pltpu.CompilerParams(
            collective_id=0, has_side_effects=True, vmem_limit_bytes=58 * 2**20
        ),
        cost_estimate=pl.CostEstimate(flops=12 * 2**30, bytes_accessed=8 * 2**20, transcendentals=2**19),
    )(grad_out, gate_pre, up_pre, weight, block_mask)


def solution(mesh):
    placed = (P("col", "row"), P("col", "row"), P("row", "col"), P("row", "col"), P("row", "col"))
    return jax.shard_map(
        shards,
        mesh=mesh,
        in_specs=placed,
        out_specs=(P("row", "col"), P("col", "row"), P("col", "row"), P("row", "col")),
        check_vma=False,
    )
```

time: 443 us -> 121 us (0.27)
  waiting for transfers between devices: 391 us -> 0 us
  Pallas kernels: 0 us -> 115 us
  matrix products: 30.7 us -> 0 us
  between operations: 13.8 us -> 0.66 us
    reduce_scatter x2 -> x0, waiting for transfers between devices: 251 us -> none  [the longest x1 218 us: shards(): lax.psum_scatter(contract(left, masked, 1, 0).astype(jnp.bfloat16), 'row'...]
    all_gather x2 -> x0, waiting for transfers between devices: 139 us -> none  [the longest x1 103 us: shards(): all_grads = lax.all_gather(grad_out, 'row', axis=0, tiled=True)]
    pallas_call x0 -> x1, Pallas kernels: none -> 115 us  [shards(): pl.pallas_call(kernel, out_shape=(jax.ShapeDtypeStruct((SHARD, 1024), BF1...]
    dot_general x3 -> x0, matrix products: 30.7 us -> none  [contract(): lax.dot_general(left, right, (((left_dim,), (right_dim,)), ((), ())), pre...]
  transfers between devices with their start and end apart: 4 -> 0, of which waited for: 4 -> 0; matrix products, arithmetic and copies ran while one was open for 3% -> 0% of each run, Pallas kernels for 0% -> 0%
where the time goes in v2:
time: 121 us; the launch traced here: 120 us
  Pallas kernels  115 us (95%)
  local copies, waits for them, and re-layouts  4.32 us (4%)
    pallas_call x1, Pallas kernels, shards(): pl.pallas_call(kernel, out_shape=(jax.ShapeDtypeStruct((SHARD, 1024), BF1...  115 us
    unnamed x10, local copies, waits for them, and re-layouts  4.32 us

profile of v2, /device:TPU:8, one launch (start us, length us, event | category | flops | bytes accessed | tf_op | source)
XLA Modules:
  0.0 120.5 jit_solution(11650031725828030940)
XLA Ops:
  0.6 115.5 %shard_map.84 = (bf16[128,1024]{1,0:T(8,128)(2,1)}, bf16[512,512]{1,0:T(8,128)(2,1)}, bf16[512,512]{1,0:T(8,128)(2,1)}, bf16[512,1024]{1,0:T(8,128)(2,1)}) custom-call(bf16[128,1024]{1,0:T(8,128)(2,1)} %grad_ref.1, bf16[512,512]{1,0:T(8,128)(2,1)} %gate_ref.1, bf16[512,512]{1,0:T(8,128)(2,1)} %up_ref.1, bf16[512,1024]{1,0:T(8,128)(2,1)} %weight_ref.1, ...), custom_call_target="tpu_custom_call" | custom-call | flops 12884901888 | bytes 8388608 | tf_op jit(solution)/shard_map/pallas_call | solution.py:519
  116.1 0.0 copy-start.2
  116.1 0.0 copy-start.1
  116.1 1.8 %copy.13 = bf16[128,1024]{1,0:T(8,128)(2,1)} copy(bf16[128,1024]{1,0:T(8,128)(2,1)} %get-tuple-element.8) | data formatting | bytes 524288
  117.9 0.0 copy-done.2
  117.9 0.0 copy-start
  117.9 0.8 copy.14
  118.7 0.0 copy-done.1
  118.7 0.8 copy.15
  119.5 0.0 copy-done
  119.5 1.0 copy.16
Async XLA Ops:
  116.1 1.8 %copy-start.2 = (bf16[512,512]{1,0:T(8,128)(2,1)S(1)}, bf16[512,512]{1,0:T(8,128)(2,1)}, u32[]{:S(2)}) copy-start(bf16[512,512]{1,0:T(8,128)(2,1)} %get-tuple-element.9) | copy-start | bytes 1572868
  116.1 2.6 %copy-start.1 = (bf16[512,512]{1,0:T(8,128)(2,1)S(1)}, bf16[512,512]{1,0:T(8,128)(2,1)}, u32[]{:S(2)}) copy-start(bf16[512,512]{1,0:T(8,128)(2,1)} %get-tuple-element.10) | copy-start | bytes 1572868
  117.9 1.6 %copy-start = (bf16[512,1024]{1,0:T(8,128)(2,1)S(1)}, bf16[512,1024]{1,0:T(8,128)(2,1)}, u32[]{:S(2)}) copy-start(bf16[512,1024]{1,0:T(8,128)(2,1)} %get-tuple-element.11) | copy-start | bytes 3145732

commit v3 on v2

--- a/solution.py
+++ b/solution.py
@@ -7,12 +7,11 @@
 
 NZ, NX, NY = 8, 4, 4
 SHARD = 128
-CUT = 32
+CUT = 48
 REST = SHARD - CUT
 MESH = pl.DeviceIdType.MESH
 F32 = jnp.float32
 BF16 = jnp.bfloat16
-ORDER = (4, 3, -3, 2, -2, 1, -1, 0)
 
 
 class Slots:
@@ -164,16 +163,21 @@
         arrive(gb(0, 1), "gbx")
         bz_first(1)
 
-    def bz(k, e):
+    def bzo(o, e):
         low, high = (-4, 3) if e == 0 else (-3, 4)
-        for o in (-k, k):
-            if o < low or o > high:
-                continue
-            arrive(gb(o, e), "gbz", e, o)
-            if o < 0 and o > low:
-                send(gb(o, e), gb(o, e), zdev(1), "gbz", e, o - 1)
-            if o > 0 and o < high:
-                send(gb(o, e), gb(o, e), zdev(-1), "gbz", e, o + 1)
+        arrive(gb(o, e), "gbz", e, o)
+        if o < 0 and o > low:
+            send(gb(o, e), gb(o, e), zdev(1), "gbz", e, o - 1)
+        if o > 0 and o < high:
+            send(gb(o, e), gb(o, e), zdev(-1), "gbz", e, o + 1)
+
+    def hx_out():
+        for s in (0, 1):
+            send(hx, hall.at[1 + s, col], mates[s], "hx", s)
+
+    def hx_in():
+        for s in (0, 1):
+            arrive(hall.at[1 + s, col], "hx", s)
 
     def h0(f):
         for h in (0, 1):
@@ -205,39 +209,31 @@
     def mm_part(o):
         block = zi(o)
         for s in (0, 1):
-            @pl.loop(0, 2)
-            def _(n):
-                at = tile(n, 256)
-                part[block, :, pl.ds(pl.multiple_of(s * 512 + n * 256, 256), 256)] = (
-                    dot(hall[0, block], wm[s, :, at], 1, 0) + dot(hall[1 + s, block], wo[s, :, at], 1, 0)
-                ).astype(BF16)
-
-    def mm_dpart(block):
-        @pl.loop(0, 2)
-        def _(n):
-            at = tile(n, 256)
-            first, second = gall[block, :, pl.ds(0, 512)], gall[block, :, pl.ds(512, 512)]
-            dpart[1, block, :, at] = dot(first, wo[0, at, :], 1, 1).astype(BF16)
-            dpart[2, block, :, at] = dot(second, wo[1, at, :], 1, 1).astype(BF16)
-            dpart[0, block, :, at] = (dot(first, wm[0, at, :], 1, 1) + dot(second, wm[1, at, :], 1, 1)).astype(BF16)
-
-    def mm_weight(k):
-        pair = pl.ds(2 * k, 2)
-
-        def gsum(dst, at, f, cols):
+            part[block, :, pl.ds(s * 512, 512)] = (
+                dot(hall[0, block], wm[s], 1, 0) + dot(hall[1 + s, block], wo[s], 1, 0)
+            ).astype(BF16)
+
+    def mm_dpart(f, block):
+        first, second = gall[block, :, pl.ds(0, 512)], gall[block, :, pl.ds(512, 512)]
+        if f == 0:
+            product = dot(first, wm[0], 1, 1) + dot(second, wm[1], 1, 1)
+        else:
+            product = dot((first, second)[f - 1], wo[f - 1], 1, 1)
+        dpart[f, block] = product.astype(BF16)
+
+    def mm_sum(dst, f, s):
+        for k in (0, 1):
+            blocks = pl.ds(4 * k, 4)
             product = dot(
-                hall[f, pair].reshape(512, 512), gall[pair, :, cols].reshape(512, 256), 0, 0
+                hall[f, blocks].reshape(1024, 512), gall[blocks, :, pl.ds(s * 512, 512)].reshape(1024, 512), 0, 0
             )
-            dst[:, at] = product if k == 0 else dst[:, at] + product
-
-        for s in (0, 1):
-            @pl.loop(0, 2)
-            def _(n):
-                gsum(accx.at[s], tile(n, 256), 1 + s, pl.ds(pl.multiple_of(s * 512 + n * 256, 256), 256))
-
-        @pl.loop(0, 4)
-        def _(n):
-            gsum(acc, tile(n, 256), 0, tile(n, 256))
+            dst[...] = product if k == 0 else dst[...] + product
+
+    def mm_mate(s):
+        mm_sum(accx.at[s], 1 + s, s)
+
+    def mm_own(s):
+        mm_sum(acc.at[s], 0, s)
 
     def pa(o, e):
         return rows_a(part, o, e)
@@ -275,32 +271,31 @@
         else:
             send(held, la("pz", o + 1, 1), zdev(-1), "pz", o + 1, 1)
 
-    def rz(o):
-        for e in (1, 0):
-            sides = []
-            if 0 <= o < 4 and not (o == 3 and e == 1):
-                sides.append(-1)
-            if -4 < o <= 0 and not (o == -3 and e == 0):
-                sides.append(1)
-            terms = [pb(o, e)]
-            for side in sides:
-                held = lb("pbz", e, o, side)
-                arrive(held, "pbz", e, o, side)
-                terms.append(held)
-            src = terms[-1]
-            if len(terms) > 1:
-                add(src, REST, *terms)
-            if o == 4:
-                if e == 0:
-                    send(src, lb("pbz", e, 3, -1), zdev(1), "pbz", e, 3, -1)
-                else:
-                    send(src, lb("pbz", e, -3, 1), zdev(-1), "pbz", e, -3, 1)
-            elif o > 0:
-                send(src, lb("pbz", e, o - 1, -1), zdev(1), "pbz", e, o - 1, -1)
-            elif o < 0:
-                send(src, lb("pbz", e, o + 1, 1), zdev(-1), "pbz", e, o + 1, 1)
-            elif e == 1:
-                send(src, lb("pbx"), across, "pbx")
+    def rz(o, e):
+        sides = []
+        if 0 <= o < 4 and not (o == 3 and e == 1):
+            sides.append(-1)
+        if -4 < o <= 0 and not (o == -3 and e == 0):
+            sides.append(1)
+        terms = [pb(o, e)]
+        for side in sides:
+            held = lb("pbz", e, o, side)
+            arrive(held, "pbz", e, o, side)
+            terms.append(held)
+        src = terms[-1]
+        if len(terms) > 1:
+            add(src, REST, *terms)
+        if o == 4:
+            if e == 0:
+                send(src, lb("pbz", e, 3, -1), zdev(1), "pbz", e, 3, -1)
+            else:
+                send(src, lb("pbz", e, -3, 1), zdev(-1), "pbz", e, -3, 1)
+        elif o > 0:
+            send(src, lb("pbz", e, o - 1, -1), zdev(1), "pbz", e, o - 1, -1)
+        elif o < 0:
+            send(src, lb("pbz", e, o + 1, 1), zdev(-1), "pbz", e, o + 1, 1)
+        elif e == 1:
+            send(src, lb("pbx"), across, "pbx")
 
     def bf():
         held = lb("pbx")
@@ -309,7 +304,7 @@
 
     S = {2: 0, -1: 1, 1: 2, 0: 3}
     Y = {("m", -1): 0, ("m", 1): 1, (-1, 0): 2, (-1, 1): 3, (1, 0): 4, (1, 1): 5}
-    FS = (1, 2, 0)
+    DYS = (2, -1, 1, 0)
 
     def own(dy):
         return yi(dy) * 2 + core
@@ -320,15 +315,18 @@
     def ly(f, *key):
         return land_y.at[f, Y[key]]
 
-    def dsib(dy):
-        block = yi(dy) * 2 + (1 - core)
-        mm_dpart(block)
-        for f in FS:
+    def dsib(f):
+        for dy in DYS:
+            block = yi(dy) * 2 + (1 - core)
+            mm_dpart(f, block)
             send(dpart.at[f, block], land_s.at[f, S[dy]], sibling, "ds", f, dy)
-        mm_dpart(own(dy))
-
-    def dadd(dy):
-        for f in FS:
+
+    def down(f):
+        for dy in DYS:
+            mm_dpart(f, own(dy))
+
+    def dadd(f):
+        for dy in DYS:
             held = land_s.at[f, S[dy]]
             arrive(held, "ds", f, dy)
             here = dpart.at[f, own(dy)]
@@ -418,96 +416,127 @@
         @pl.loop(0, 4)
         def _(i):
             for j in range(8):
-                cols = pl.ds(j * 128, 128)
-                total = acc[tile(i, 128), cols] + wrecv[j // 4, tile(i, 128), pl.ds(j % 4 * 128, 128)].astype(F32)
-                dweight_ref[tile(i, 128), cols] = (total * keep(i, j)).astype(BF16)
-
-    bz_first(0)
+                at = (j // 4, tile(i, 128), pl.ds(j % 4 * 128, 128))
+                dweight_ref[tile(i, 128), pl.ds(j * 128, 128)] = (
+                    (acc[at] + wrecv[at].astype(F32)) * keep(i, j)
+                ).astype(BF16)
+
+    send(gb(0, 0), gb(0, 0), across, "gbx")
+    hx_out()
     az_next(0)
-    for s in (0, 1):
-        send(hx, hall.at[1 + s, col], mates[s], "hx", s)
-    send(gb(0, 0), gb(0, 0), across, "gbx")
-    h0(0)
     ax_send(0)
     mask_weights()
-    h1(0)
-    bz(1, 0)
-    for s in (0, 1):
-        arrive(hall.at[1 + s, col], "hx", s)
-    h0(1)
-    h0(2)
-    az(-1, 1)
-    h2(0)
-    h3(0)
+    bz_first(0)
+    h0(0)
+    az(1)
+    az(-1)
     bx()
     weights_out()
-    bz(2, 0)
+    h1(0)
+    bzo(1, 0)
+    bzo(-1, 0)
+    h2(0)
+    az(-2)
+    az(2)
+    hx_in()
+    h0(2)
+    h0(1)
+    h3(0)
+    ax(0)
+    bzo(1, 1)
+    bzo(-1, 1)
+    h4(0)
+    ax(1)
+    h1(2)
+    bzo(2, 0)
+    bzo(-2, 0)
+    ax(-1)
+    az(-3)
+    az(3)
+    h2(2)
     h1(1)
-    bz(1, 1)
+    bzo(-2, 1)
+    bzo(2, 1)
     h2(1)
-    az(-2, 2)
+    bzo(3, 0)
+    bzo(-3, 0)
+    h3(2)
+    az(-4)
+    weights_in()
+    bzo(3, 1)
+    h4(2)
+    ax(-2)
     h3(1)
-    bz(3, 0)
-    h1(2)
-    h2(2)
-    bz(2, 1)
-    az(-3, 3)
-    h3(2)
-    weights_in()
-    for f in (0, 1, 2):
-        h4(f)
-    mm_part(ORDER[0])
-    bz(4, 0)
-    mm_part(ORDER[1])
-    bz(3, 1)
-    mm_part(ORDER[2])
-    xs(ORDER[0])
-    rz(ORDER[0])
-    az(-4)
-    bz(4, 1)
-    mm_part(ORDER[3])
-    xs(ORDER[1])
-    ax(0, -1, 1, -2, 2, -3, 3, -4)
-
-    def tick(t):
-        if 1 <= t < 7:
-            xs(ORDER[t + 1])
-        if 1 <= t <= 7:
-            rz(ORDER[t])
-        if 1 <= t <= 8:
-            zf(ORDER[t - 1])
-        if t + 3 < 8 and t >= 1:
-            mm_part(ORDER[t + 3])
-
+    bzo(-3, 1)
+    ax(2)
+    h4(1)
+    mm_part(-1)
+    mm_part(3)
+    rz(3, 1)
+    mm_part(4)
+    xs(4)
+    mm_part(-3)
+    rz(-3, 0)
+    mm_part(1)
+    bzo(4, 1)
+    xs(1)
+    xs(-3)
+    ax(-3)
+    mm_part(2)
+    xs(2)
+    ax(3)
+    xs(3)
+    mm_part(-2)
+    rz(4, 1)
+    mm_part(0)
+    xs(0)
+    rz(4, 0)
+    xs(-2)
+    bzo(-4, 0)
+    xs(-1)
+    ax(-4)
     dsib(2)
-    tick(1)
-    dsib(-1)
+    mm_mate(1)
+    zf(4)
+    down(2)
+    dsib(1)
     dadd(2)
-    tick(2)
-    dsib(1)
-    dadd(-1)
-    tick(3)
+    down(1)
+    rz(-3, 1)
+    zf(-3)
+    rz(2, 1)
+    rz(3, 0)
     dadd(1)
+    dsib(0)
+    down(0)
+    mm_mate(0)
+    dweights_out()
+    rz(-2, 1)
+    zf(3)
+    dmid(2)
+    rz(1, 1)
+    mm_own(0)
+    zf(-2)
+    rz(-2, 0)
     dmid(1)
-    dsib(0)
-    tick(4)
-    dmid(2)
+    rz(2, 0)
     dadd(0)
+    mm_own(1)
+    rz(-1, 1)
+    zf(2)
+    zf(-1)
+    dmate(2)
+    dmate(1)
+    rz(-1, 0)
+    rz(1, 0)
     dmid(0)
-    mm_weight(0)
-    mm_weight(1)
-    tick(5)
-    mm_weight(2)
-    mm_weight(3)
-    dweights_out()
-    dmate(1)
-    tick(6)
-    dmate(2)
-    tick(7)
+    dweights_in()
+    rz(0, 1)
+    zf(1)
     grads_own()
-    dweights_in()
     grads_mates()
-    tick(8)
+    zf(0)
+    rz(0, 0)
     bf()
 
     for copy in sends:
@@ -534,7 +563,7 @@
             pltpu.VMEM((2, 512, 512), BF16),
             pltpu.VMEM((2, 512, 512), BF16),
             pltpu.VMEM((3, 8, 256, 512), BF16),
-            pltpu.VMEM((512, 1024), F32),
+            pltpu.VMEM((2, 512, 512), F32),
             pltpu.VMEM((2, 512, 512), F32),
             pltpu.VMEM((2, 512, 512), BF16),
             pltpu.VMEM((2, 512, 512), BF16),

time: 121 us -> 94.8 us (0.78)
  Pallas kernels: 115 us -> 89.6 us
    pallas_call x1, Pallas kernels: 115 us -> 89.6 us  [shards(): pl.pallas_call(kernel, out_shape=(jax.ShapeDtypeStruct((SHARD, 1024), BF1...]
where the time goes in v3:
time: 94.8 us; the launch traced here: 94.6 us
  Pallas kernels  89.6 us (95%)
  local copies, waits for them, and re-layouts  4.32 us (5%)
    pallas_call x1, Pallas kernels, shards(): pl.pallas_call(kernel, out_shape=(jax.ShapeDtypeStruct((SHARD, 1024), BF1...  89.6 us
    unnamed x10, local copies, waits for them, and re-layouts  4.32 us

profile of v3, /device:TPU:8, one launch (start us, length us, event | category | flops | bytes accessed | tf_op | source)
XLA Modules:
  0.0 94.6 jit_solution(17194026919773655714)
XLA Ops:
  0.6 89.6 %shard_map.84 = (bf16[128,1024]{1,0:T(8,128)(2,1)}, bf16[512,512]{1,0:T(8,128)(2,1)}, bf16[512,512]{1,0:T(8,128)(2,1)}, bf16[512,1024]{1,0:T(8,128)(2,1)}) custom-call(bf16[128,1024]{1,0:T(8,128)(2,1)} %grad_ref.1, bf16[512,512]{1,0:T(8,128)(2,1)} %gate_ref.1, bf16[512,512]{1,0:T(8,128)(2,1)} %up_ref.1, bf16[512,1024]{1,0:T(8,128)(2,1)} %weight_ref.1, ...), custom_call_target="tpu_custom_call" | custom-call | flops 12884901888 | bytes 8388608 | tf_op jit(solution)/shard_map/pallas_call | solution.py:548
  90.3 0.0 copy-start.2
  90.3 0.0 copy-start.1
  90.3 1.8 %copy.13 = bf16[128,1024]{1,0:T(8,128)(2,1)} copy(bf16[128,1024]{1,0:T(8,128)(2,1)} %get-tuple-element.8) | data formatting | bytes 524288
  92.1 0.0 copy-done.2
  92.1 0.0 copy-start
  92.1 0.8 copy.14
  92.9 0.0 copy-done.1
  92.9 0.8 copy.15
  93.7 0.0 copy-done
  93.7 1.0 %copy.16 = bf16[512,1024]{1,0:T(8,128)(2,1)} copy(bf16[512,1024]{1,0:T(8,128)(2,1)S(1)} %copy-done) | data formatting | bytes 2097152
Async XLA Ops:
  90.3 1.8 %copy-start.2 = (bf16[512,512]{1,0:T(8,128)(2,1)S(1)}, bf16[512,512]{1,0:T(8,128)(2,1)}, u32[]{:S(2)}) copy-start(bf16[512,512]{1,0:T(8,128)(2,1)} %get-tuple-element.9) | copy-start | bytes 1572868
  90.3 2.6 %copy-start.1 = (bf16[512,512]{1,0:T(8,128)(2,1)S(1)}, bf16[512,512]{1,0:T(8,128)(2,1)}, u32[]{:S(2)}) copy-start(bf16[512,512]{1,0:T(8,128)(2,1)} %get-tuple-element.10) | copy-start | bytes 1572868
  92.1 1.6 %copy-start = (bf16[512,1024]{1,0:T(8,128)(2,1)S(1)}, bf16[512,1024]{1,0:T(8,128)(2,1)}, u32[]{:S(2)}) copy-start(bf16[512,1024]{1,0:T(8,128)(2,1)} %get-tuple-element.11) | copy-start | bytes 3145732

commit v4 on v3

--- a/solution.py
+++ b/solution.py
@@ -7,8 +7,7 @@
 
 NZ, NX, NY = 8, 4, 4
 SHARD = 128
-CUT = 48
-REST = SHARD - CUT
+GCUT, PCUT = 32, 48
 MESH = pl.DeviceIdType.MESH
 F32 = jnp.float32
 BF16 = jnp.bfloat16
@@ -31,8 +30,9 @@
 
 
 def kernel(
-    grad_ref, gate_ref, up_ref, weight_ref, mask_ref,
-    out_ref, dgate_ref, dup_ref, dweight_ref,
+    grad_in, gate_in, up_in, weight_in, mask_ref,
+    out_to, dgate_to, dup_to, dweight_to,
+    gate_ref, up_ref, weight_ref, out_ref, dgate_ref, dup_ref, dweight_ref, in_sem, out_sem,
     gall, hall, hx, part, wm, wo, dpart, acc, accx, wsend, wrecv,
     land_a, land_b, land_s, land_y, land_x,
     send_sem, recv_sem,
@@ -96,10 +96,17 @@
         pl.semaphore_signal(barrier, inc=1, device_id=dev, device_id_type=MESH)
 
     mine, other = x // 2, 1 - x // 2
-
-    @pl.loop(0, SHARD // 16)
-    def _(i):
-        gall[z, pl.ds(pl.multiple_of(mine * SHARD + i * 16, 16), 16), :] = grad_ref[tile(i, 16), :]
+    taken = {}
+    for n, (name, src, dst) in enumerate((
+        ("grad", grad_in, gall.at[z, pl.ds(pl.multiple_of(mine * SHARD, SHARD), SHARD), :]),
+        ("gate", gate_in, gate_ref),
+        ("up", up_in, up_ref),
+        ("weight", weight_in, weight_ref),
+    )):
+        taken[name] = pltpu.make_async_copy(src, dst, in_sem.at[n])
+        taken[name].start()
+    results = ((out_ref, out_to), (dgate_ref, dgate_to), (dup_ref, dup_to), (dweight_ref, dweight_to))
+    given = [pltpu.make_async_copy(src, dst, out_sem.at[n]) for n, (src, dst) in enumerate(results)]
 
     def hidden_into(dst, which):
         for j in (0, 1):
@@ -112,22 +119,17 @@
                     g * jax.nn.sigmoid(g) * u
                 ).astype(BF16)
 
-    hidden_into(hx, 1 - parity)
-    hidden_into(hall.at[0, col], parity)
-
     pl.semaphore_wait(barrier, 8)
-
-    def rows_a(buf, o, e):
-        return buf.at[zi(o), pl.ds(pl.multiple_of((other if e else mine) * SHARD, 16), CUT), :]
-
-    def rows_b(buf, o, e):
-        return buf.at[zi(o), pl.ds(pl.multiple_of((other if e else mine) * SHARD + CUT, 16), REST), :]
+    taken["grad"].wait()
+
+    def rows(buf, o, e, start, size):
+        return buf.at[zi(o), pl.ds(pl.multiple_of((other if e else mine) * SHARD + start, 16), size), :]
 
     def ga(o, e):
-        return rows_a(gall, o, e)
+        return rows(gall, o, e, 0, GCUT)
 
     def gb(o, e):
-        return rows_b(gall, o, e)
+        return rows(gall, o, e, GCUT, SHARD - GCUT)
 
     def hid(f, dy, h=None):
         at = slice(None) if h is None else pl.ds(h * 128, 128)
@@ -236,10 +238,10 @@
         mm_sum(acc.at[s], 0, s)
 
     def pa(o, e):
-        return rows_a(part, o, e)
+        return rows(part, o, e, 0, PCUT)
 
     def pb(o, e):
-        return rows_b(part, o, e)
+        return rows(part, o, e, PCUT, SHARD - PCUT)
 
     def la(*key):
         return land_a.at[slot_a(*key)]
@@ -263,9 +265,9 @@
             arrive(la("pz", o, side), "pz", o, side)
             terms.append(la("pz", o, side))
         if o == 0:
-            add(out_ref.at[pl.ds(0, CUT), :], CUT, *terms)
+            add(out_ref.at[pl.ds(0, PCUT), :], PCUT, *terms)
             return
-        add(held, CUT, *terms)
+        add(held, PCUT, *terms)
         if o > 0:
             send(held, la("pz", o - 1, -1), zdev(1), "pz", o - 1, -1)
         else:
@@ -284,7 +286,7 @@
             terms.append(held)
         src = terms[-1]
         if len(terms) > 1:
-            add(src, REST, *terms)
+            add(src, SHARD - PCUT, *terms)
         if o == 4:
             if e == 0:
                 send(src, lb("pbz", e, 3, -1), zdev(1), "pbz", e, 3, -1)
@@ -300,7 +302,7 @@
     def bf():
         held = lb("pbx")
         arrive(held, "pbx")
-        add(out_ref.at[pl.ds(CUT, REST), :], REST, lb("pbz", 0, 0, 1), held)
+        add(out_ref.at[pl.ds(PCUT, SHARD - PCUT), :], SHARD - PCUT, lb("pbz", 0, 0, 1), held)
 
     S = {2: 0, -1: 1, 1: 2, 0: 3}
     Y = {("m", -1): 0, ("m", 1): 1, (-1, 0): 2, (-1, 1): 3, (1, 0): 4, (1, 1): 5}
@@ -422,11 +424,16 @@
                 ).astype(BF16)
 
     send(gb(0, 0), gb(0, 0), across, "gbx")
+    az_next(0)
+    bz_first(0)
+    taken["weight"].wait()
+    mask_weights()
+    taken["gate"].wait()
+    taken["up"].wait()
+    hidden_into(hx, 1 - parity)
     hx_out()
-    az_next(0)
     ax_send(0)
-    mask_weights()
-    bz_first(0)
+    hidden_into(hall.at[0, col], parity)
     h0(0)
     az(1)
     az(-1)
@@ -435,117 +442,136 @@
     h1(0)
     bzo(1, 0)
     bzo(-1, 0)
+    az(2)
+    az(-2)
     h2(0)
-    az(-2)
-    az(2)
     hx_in()
+    h0(1)
     h0(2)
-    h0(1)
     h3(0)
     ax(0)
     bzo(1, 1)
     bzo(-1, 1)
+    ax(1)
     h4(0)
-    ax(1)
-    h1(2)
+    ax(-1)
+    h1(1)
     bzo(2, 0)
     bzo(-2, 0)
-    ax(-1)
     az(-3)
     az(3)
-    h2(2)
-    h1(1)
+    h2(1)
+    h1(2)
     bzo(-2, 1)
     bzo(2, 1)
-    h2(1)
+    h2(2)
+    weights_in()
+    bzo(-3, 0)
     bzo(3, 0)
-    bzo(-3, 0)
+    ax(2)
+    h3(1)
+    az(-4)
+    ax(-2)
+    h4(1)
+    ax(-3)
     h3(2)
-    az(-4)
-    weights_in()
     bzo(3, 1)
+    ax(3)
+    bzo(-3, 1)
     h4(2)
-    ax(-2)
-    h3(1)
-    bzo(-3, 1)
-    ax(2)
-    h4(1)
+    mm_part(4)
+    rz(4, 0)
+    mm_part(3)
+    ax(-4)
+    mm_part(0)
+    xs(0)
+    mm_part(1)
+    rz(4, 1)
+    xs(4)
+    mm_part(-2)
+    xs(-2)
+    bzo(-4, 0)
+    xs(1)
+    rz(3, 1)
     mm_part(-1)
-    mm_part(3)
-    rz(3, 1)
-    mm_part(4)
-    xs(4)
+    xs(-1)
+    xs(3)
     mm_part(-3)
     rz(-3, 0)
-    mm_part(1)
     bzo(4, 1)
-    xs(1)
-    xs(-3)
-    ax(-3)
-    mm_part(2)
-    xs(2)
-    ax(3)
-    xs(3)
-    mm_part(-2)
-    rz(4, 1)
-    mm_part(0)
-    xs(0)
-    rz(4, 0)
-    xs(-2)
-    bzo(-4, 0)
-    xs(-1)
-    ax(-4)
     dsib(2)
-    mm_mate(1)
-    zf(4)
     down(2)
     dsib(1)
-    dadd(2)
     down(1)
     rz(-3, 1)
-    zf(-3)
+    zf(4)
+    dadd(2)
+    xs(-3)
+    mm_part(2)
     rz(2, 1)
+    xs(2)
+    dadd(1)
+    rz(-2, 0)
     rz(3, 0)
-    dadd(1)
-    dsib(0)
-    down(0)
+    mm_mate(1)
     mm_mate(0)
     dweights_out()
-    rz(-2, 1)
     zf(3)
     dmid(2)
     rz(1, 1)
+    rz(-2, 1)
+    dsib(0)
+    rz(-1, 0)
+    zf(-3)
+    down(0)
+    rz(2, 0)
+    dmid(1)
     mm_own(0)
-    zf(-2)
-    rz(-2, 0)
-    dmid(1)
-    rz(2, 0)
+    zf(2)
     dadd(0)
+    rz(-1, 1)
     mm_own(1)
-    rz(-1, 1)
-    zf(2)
-    zf(-1)
     dmate(2)
     dmate(1)
-    rz(-1, 0)
     rz(1, 0)
+    zf(-2)
+    zf(1)
     dmid(0)
     dweights_in()
+    given[3].start()
     rz(0, 1)
-    zf(1)
+    zf(-1)
+    rz(0, 0)
+    grads_mates()
     grads_own()
-    grads_mates()
+    given[1].start()
+    given[2].start()
     zf(0)
-    rz(0, 0)
     bf()
+    given[0].start()
 
     for copy in sends:
         copy.wait_send()
+    for copy in given:
+        copy.wait()
+
+
+def hand_on(*refs):
+    sources, targets, held, sem = refs[:4], refs[4:8], refs[8:12], refs[12]
+    ins = [pltpu.make_async_copy(a, b, sem.at[0, n]) for n, (a, b) in enumerate(zip(sources, held))]
+    outs = [pltpu.make_async_copy(a, b, sem.at[1, n]) for n, (a, b) in enumerate(zip(held, targets))]
+    for copy in ins:
+        copy.start()
+    for first, then in zip(ins, outs):
+        first.wait()
+        then.start()
+    for copy in outs:
+        copy.wait()
 
 
 def shards(gate_pre, up_pre, weight, block_mask, grad_out):
-    vmem = pl.BlockSpec(memory_space=pltpu.VMEM)
-    return pl.pallas_call(
+    anywhere = pl.BlockSpec(memory_space=pl.ANY)
+    results = pl.pallas_call(
         kernel,
         out_shape=(
             jax.ShapeDtypeStruct((SHARD, 1024), BF16),
@@ -553,9 +579,18 @@
             jax.ShapeDtypeStruct((512, 512), BF16),
             jax.ShapeDtypeStruct((512, 1024), BF16),
         ),
-        in_specs=[vmem] * 4 + [pl.BlockSpec(memory_space=pltpu.SMEM)],
-        out_specs=[vmem] * 4,
+        in_specs=[anywhere] * 4 + [pl.BlockSpec(memory_space=pltpu.SMEM)],
+        out_specs=[anywhere] * 4,
         scratch_shapes=[
+            pltpu.VMEM((512, 512), BF16),
+            pltpu.VMEM((512, 512), BF16),
+            pltpu.VMEM((512, 1024), BF16),
+            pltpu.VMEM((SHARD, 1024), BF16),
+            pltpu.VMEM((512, 512), BF16),
+            pltpu.VMEM((512, 512), BF16),
+            pltpu.VMEM((512, 1024), BF16),
+            pltpu.SemaphoreType.DMA((4,)),
+            pltpu.SemaphoreType.DMA((4,)),
             pltpu.VMEM((NZ, 256, 1024), BF16),
             pltpu.VMEM((3, 8, 256, 512), BF16),
             pltpu.VMEM((256, 512), BF16),
@@ -567,8 +602,8 @@
             pltpu.VMEM((2, 512, 512), F32),
             pltpu.VMEM((2, 512, 512), BF16),
             pltpu.VMEM((2, 512, 512), BF16),
-            pltpu.VMEM((15, CUT, 1024), BF16),
-            pltpu.VMEM((15, REST, 1024), BF16),
+            pltpu.VMEM((15, PCUT, 1024), BF16),
+            pltpu.VMEM((15, SHARD - PCUT, 1024), BF16),
             pltpu.VMEM((3, 4, 256, 512), BF16),
             pltpu.VMEM((3, 6, 128, 512), BF16),
             pltpu.VMEM((2, 256, 512), BF16),
@@ -580,6 +615,13 @@
         ),
         cost_estimate=pl.CostEstimate(flops=12 * 2**30, bytes_accessed=8 * 2**20, transcendentals=2**19),
     )(grad_out, gate_pre, up_pre, weight, block_mask)
+    return pl.pallas_call(
+        hand_on,
+        out_shape=[jax.ShapeDtypeStruct(r.shape, r.dtype) for r in results],
+        in_specs=[anywhere] * 4,
+        out_specs=[anywhere] * 4,
+        scratch_shapes=[pltpu.VMEM(r.shape, r.dtype) for r in results] + [pltpu.SemaphoreType.DMA((2, 4))],
+    )(*results)
 
 
 def solution(mesh):

time: 94.8 us -> 90.5 us (0.955); the launches traced: 94.6 us -> 89.2 us
  local copies, waits for them, and re-layouts: 4.32 us -> 0 us
  Pallas kernels: 89.6 us -> 88.5 us
    unnamed x10 -> x0, local copies, waits for them, and re-layouts: 4.32 us -> none
    pallas_call x1, Pallas kernels: 89.6 us -> 85.8 us  [shards(): pl.pallas_call(kernel, out_shape=(jax.ShapeDtypeStruct((SHARD, 1024), BF1...]
    pallas_call x0 -> x1, Pallas kernels: none -> 2.67 us  [shards(): pl.pallas_call(hand_on, out_shape=[jax.ShapeDtypeStruct(r.shape, r.dtype)...]
where the time goes in v4:
time: 90.5 us; the launch traced here: 89.2 us
  Pallas kernels  88.5 us (98%)
    pallas_call x1, Pallas kernels, shards(): pl.pallas_call(kernel, out_shape=(jax.ShapeDtypeStruct((SHARD, 1024), BF1...  85.8 us
    pallas_call x1, Pallas kernels, shards(): pl.pallas_call(hand_on, out_shape=[jax.ShapeDtypeStruct(r.shape, r.dtype)...  2.67 us

profile of v4, /device:TPU:8, one launch (start us, length us, event | category | flops | bytes accessed | tf_op | source)
XLA Modules:
  0.0 89.2 jit_solution(3466043657840251469)
XLA Ops:
  0.6 85.8 %shard_map.84 = (bf16[128,1024]{1,0:T(8,128)(2,1)}, bf16[512,512]{1,0:T(8,128)(2,1)}, bf16[512,512]{1,0:T(8,128)(2,1)}, bf16[512,1024]{1,0:T(8,128)(2,1)}) custom-call(bf16[128,1024]{1,0:T(8,128)(2,1)} %grad_in.1, bf16[512,512]{1,0:T(8,128)(2,1)} %gate_in.1, bf16[512,512]{1,0:T(8,128)(2,1)} %up_in.1, bf16[512,1024]{1,0:T(8,128)(2,1)} %weight_in.1, ...), custom_call_target="tpu_custom_call" | custom-call | flops 12884901888 | bytes 8388608 | tf_op jit(solution)/shard_map/pallas_call | solution.py:574
  86.5 2.7 %shard_map.85 = (bf16[128,1024]{1,0:T(8,128)(2,1)}, bf16[512,512]{1,0:T(8,128)(2,1)}, bf16[512,512]{1,0:T(8,128)(2,1)}, bf16[512,1024]{1,0:T(8,128)(2,1)}) custom-call(bf16[128,1024]{1,0:T(8,128)(2,1)} %get-tuple-element.8.refs_0_, bf16[512,512]{1,0:T(8,128)(2,1)} %get-tuple-element.9.refs_1_, bf16[512,512]{1,0:T(8,128)(2,1)} %get-tuple-element.10.refs_2_, ...), custom_call_target="tpu_custom_call" | custom-call | tf_op jit(solution)/shard_map/pallas_call | solution.py:618

commit v5 on v4

--- a/solution.py
+++ b/solution.py
@@ -254,9 +254,9 @@
 
     def zf(o):
         sides = []
-        if 0 <= o < 4:
+        if 0 <= o < 3:
             sides.append(-1)
-        if -3 < o <= 0:
+        if -4 < o <= 0:
             sides.append(1)
         held = la("px", o)
         arrive(held, "px", o)
@@ -268,7 +268,9 @@
             add(out_ref.at[pl.ds(0, PCUT), :], PCUT, *terms)
             return
         add(held, PCUT, *terms)
-        if o > 0:
+        if o == 4:
+            send(held, la("pz", -3, 1), zdev(-1), "pz", -3, 1)
+        elif o > 0:
             send(held, la("pz", o - 1, -1), zdev(1), "pz", o - 1, -1)
         else:
             send(held, la("pz", o + 1, 1), zdev(-1), "pz", o + 1, 1)
@@ -423,20 +425,20 @@
                     (acc[at] + wrecv[at].astype(F32)) * keep(i, j)
                 ).astype(BF16)
 
+    az_next(0)
     send(gb(0, 0), gb(0, 0), across, "gbx")
-    az_next(0)
     bz_first(0)
-    taken["weight"].wait()
-    mask_weights()
     taken["gate"].wait()
     taken["up"].wait()
     hidden_into(hx, 1 - parity)
     hx_out()
-    ax_send(0)
     hidden_into(hall.at[0, col], parity)
     h0(0)
+    ax_send(0)
+    taken["weight"].wait()
+    mask_weights()
+    az(-1)
     az(1)
-    az(-1)
     bx()
     weights_out()
     h1(0)
@@ -452,100 +454,100 @@
     ax(0)
     bzo(1, 1)
     bzo(-1, 1)
+    ax(-1)
+    h4(0)
     ax(1)
-    h4(0)
-    ax(-1)
-    h1(1)
     bzo(2, 0)
     bzo(-2, 0)
+    h1(1)
+    az(3)
     az(-3)
-    az(3)
     h2(1)
-    h1(2)
     bzo(-2, 1)
     bzo(2, 1)
+    h1(2)
     h2(2)
+    bzo(3, 0)
+    bzo(-3, 0)
     weights_in()
-    bzo(-3, 0)
-    bzo(3, 0)
+    az(-4)
     ax(2)
     h3(1)
-    az(-4)
     ax(-2)
     h4(1)
-    ax(-3)
-    h3(2)
     bzo(3, 1)
     ax(3)
+    h3(2)
     bzo(-3, 1)
+    ax(-3)
     h4(2)
+    mm_part(-2)
+    ax(-4)
     mm_part(4)
     rz(4, 0)
-    mm_part(3)
-    ax(-4)
-    mm_part(0)
-    xs(0)
-    mm_part(1)
-    rz(4, 1)
+    xs(-2)
     xs(4)
-    mm_part(-2)
-    xs(-2)
-    bzo(-4, 0)
-    xs(1)
-    rz(3, 1)
+    mm_part(-3)
     mm_part(-1)
     xs(-1)
+    rz(4, 1)
+    mm_part(0)
+    bzo(-4, 0)
+    mm_part(3)
     xs(3)
-    mm_part(-3)
-    rz(-3, 0)
+    xs(0)
     bzo(4, 1)
-    dsib(2)
-    down(2)
     dsib(1)
     down(1)
+    dsib(2)
+    mm_mate(1)
+    zf(4)
+    dadd(1)
     rz(-3, 1)
-    zf(4)
+    rz(3, 1)
+    mm_part(1)
+    xs(1)
+    rz(3, 0)
+    rz(-3, 0)
+    down(2)
     dadd(2)
     xs(-3)
     mm_part(2)
-    rz(2, 1)
     xs(2)
-    dadd(1)
-    rz(-2, 0)
-    rz(3, 0)
-    mm_mate(1)
     mm_mate(0)
     dweights_out()
+    dmid(1)
+    rz(-2, 1)
+    rz(2, 1)
     zf(3)
-    dmid(2)
-    rz(1, 1)
-    rz(-2, 1)
     dsib(0)
-    rz(-1, 0)
     zf(-3)
     down(0)
     rz(2, 0)
-    dmid(1)
+    dmid(2)
+    rz(-2, 0)
+    mm_own(1)
+    dadd(0)
+    rz(1, 1)
+    rz(-1, 1)
     mm_own(0)
     zf(2)
-    dadd(0)
-    rz(-1, 1)
-    mm_own(1)
+    zf(-2)
+    dmate(1)
     dmate(2)
-    dmate(1)
+    rz(-1, 0)
     rz(1, 0)
-    zf(-2)
-    zf(1)
     dmid(0)
     dweights_in()
     given[3].start()
     rz(0, 1)
     zf(-1)
-    rz(0, 0)
+    zf(1)
+    grads_own()
     grads_mates()
-    grads_own()
     given[1].start()
     given[2].start()
+    rz(0, 0)
     zf(0)
     bf()
     given[0].start()
@@ -558,8 +560,14 @@
 
 def hand_on(*refs):
     sources, targets, held, sem = refs[:4], refs[4:8], refs[8:12], refs[12]
-    ins = [pltpu.make_async_copy(a, b, sem.at[0, n]) for n, (a, b) in enumerate(zip(sources, held))]
-    outs = [pltpu.make_async_copy(a, b, sem.at[1, n]) for n, (a, b) in enumerate(zip(held, targets))]
+    pieces = [(3, 0), (3, 128), (3, 256), (3, 384), (1, 0), (1, 256), (2, 0), (2, 256), (0, 0)]
+    sizes = {0: SHARD, 1: 256, 2: 256, 3: 128}
+    ins, outs = [], []
+    for n, (which, start) in enumerate(pieces):
+        at = pl.ds(start, sizes[which])
+        middle = held[which].at[at, :]
+        ins.append(pltpu.make_async_copy(sources[which].at[at, :], middle, sem.at[0, n]))
+        outs.append(pltpu.make_async_copy(middle, targets[which].at[at, :], sem.at[1, n]))
     for copy in ins:
         copy.start()
     for first, then in zip(ins, outs):
@@ -620,7 +628,7 @@
         out_shape=[jax.ShapeDtypeStruct(r.shape, r.dtype) for r in results],
         in_specs=[anywhere] * 4,
         out_specs=[anywhere] * 4,
-        scratch_shapes=[pltpu.VMEM(r.shape, r.dtype) for r in results] + [pltpu.SemaphoreType.DMA((2, 4))],
+        scratch_shapes=[pltpu.VMEM(r.shape, r.dtype) for r in results] + [pltpu.SemaphoreType.DMA((2, 9))],
     )(*results)
 
 

time: 90.5 us -> 89.8 us (level); the launches traced: 89.2 us -> 89.6 us
  no operation moved by 1% of the time
where the time goes in v5:
time: 89.8 us; the launch traced here: 89.6 us
  Pallas kernels  89 us (99%)
    pallas_call x1, Pallas kernels, shards(): pl.pallas_call(kernel, out_shape=(jax.ShapeDtypeStruct((SHARD, 1024), BF1...  86.5 us
    pallas_call x1, Pallas kernels, shards(): pl.pallas_call(hand_on, out_shape=[jax.ShapeDtypeStruct(r.shape, r.dtype)...  2.5 us

profile of v5, /device:TPU:8, one launch (start us, length us, event | category | flops | bytes accessed | tf_op | source)
XLA Modules:
  0.0 89.6 jit_solution(11666257131231797349)
XLA Ops:
  0.6 86.5 %shard_map.84 = (bf16[128,1024]{1,0:T(8,128)(2,1)}, bf16[512,512]{1,0:T(8,128)(2,1)}, bf16[512,512]{1,0:T(8,128)(2,1)}, bf16[512,1024]{1,0:T(8,128)(2,1)}) custom-call(bf16[128,1024]{1,0:T(8,128)(2,1)} %grad_in.1, bf16[512,512]{1,0:T(8,128)(2,1)} %gate_in.1, bf16[512,512]{1,0:T(8,128)(2,1)} %up_in.1, bf16[512,1024]{1,0:T(8,128)(2,1)} %weight_in.1, ...), custom_call_target="tpu_custom_call" | custom-call | flops 12884901888 | bytes 8388608 | tf_op jit(solution)/shard_map/pallas_call | solution.py:582
  87.1 2.5 %shard_map.85 = (bf16[128,1024]{1,0:T(8,128)(2,1)}, bf16[512,512]{1,0:T(8,128)(2,1)}, bf16[512,512]{1,0:T(8,128)(2,1)}, bf16[512,1024]{1,0:T(8,128)(2,1)}) custom-call(bf16[128,1024]{1,0:T(8,128)(2,1)} %get-tuple-element.8.refs_0_, bf16[512,512]{1,0:T(8,128)(2,1)} %get-tuple-element.9.refs_1_, bf16[512,512]{1,0:T(8,128)(2,1)} %get-tuple-element.10.refs_2_, ...), custom_call_target="tpu_custom_call" | custom-call | tf_op jit(solution)/shard_map/pallas_call | solution.py:626
